TPU v7x, 32 devices: a whole 2x2x4 slice. The times are simulated.
32 devices in a mesh: role: 2 (over y), band: 4 (over z), turn: 4 (over x, core).
Axes of the slice: x: 2, y: 2, z: 4, core: 2. Of those that a mesh axis runs over, the one named last changes fastest.
Arguments:
- voltages: bfloat16 [8, 2, 256, 3840], P(('role', 'band'), None, 'turn'), may hold values from -6 to 6
- station_flags: int32 [256], P('turn'), may hold values 0 or 1
- filter_taps: bfloat16 [8, 256, 256], replicated, may hold values from -0.125 to 0.125
- kernel_rows: bfloat16 [8, 1, 32, 256], P(('role', 'band')), may hold values from -0.375 to 0.375
- kernel_cols: bfloat16 [8, 1, 32, 256], P(('role', 'band')), may hold values from -0.375 to 0.375
- cell_index: int32 [2, 1024, 1], P(None, ('role', 'band', 'turn')), may hold values from 0 to 4095
Outputs:
- image: float32 [32, 128], P(('role', 'band', 'turn'))
All inputs are finite; a program needn't handle non-finite values. No bound on the sum of `station_flags` on one device may be relied on, other than what follows from the above.
Results may differ from a plain program's by a relative error of at most 0.0071.
Values may be sent and summed in bfloat16 or wider, within the bound.
No kernel may reach another device: no remote copies, remote signals or barrier semaphores. Data moves between devices by JAX's collectives and lax.ppermute only.
A program may use at most 64 MiB of HBM per device.

v0:
```python
import math

import jax
import jax.numpy as jnp
from jax import lax
from jax.sharding import PartitionSpec as P

FINE = 128
NGRID = 4096
MW = 128
ROWS_DEV = 1


def channelize(voltages, station_flags, filter_taps):
    polars, station_rows, sample_width = voltages.shape
    tap_count, two_fine, _ = filter_taps.shape
    block_total = sample_width // two_fine
    frames = block_total - tap_count + 1
    flagged = voltages * station_flags[None, :, None].astype(voltages.dtype)
    blocks = flagged.reshape(polars * station_rows, block_total, two_fine)
    running = jnp.zeros((polars * station_rows * frames, two_fine), jnp.float32)
    for tap_index in range(tap_count):
        segment = blocks[:, tap_index : tap_index + frames, :].reshape(
            polars * station_rows * frames, two_fine
        )
        running = running + jnp.dot(
            segment, filter_taps[tap_index], preferred_element_type=jnp.float32
        )
    fine_count = two_fine // 2
    result = running.astype(jnp.bfloat16).reshape(polars, station_rows, frames, 2, fine_count)
    return jnp.transpose(result, (4, 0, 1, 3, 2)).reshape(
        fine_count, polars, station_rows, 2 * frames
    )


def correlate(spectra):
    frames = spectra.shape[3] // 2
    station_count = spectra.shape[2]
    swapped = jnp.concatenate([-spectra[..., frames:], spectra[..., :frames]], axis=3)
    stacked = jnp.concatenate([spectra, swapped], axis=2)
    products = jnp.einsum("fpsa,fpka->fpsk", spectra, stacked, preferred_element_type=jnp.float32)
    stokes = (products[:, 0] + products[:, 1]) * (1.0 / frames)
    return jnp.stack([stokes[:, :, :station_count], stokes[:, :, station_count:]]).astype(
        jnp.bfloat16
    )


def subgrids(visibility, kernel_rows, kernel_cols):
    fine_local = visibility.shape[1]
    station_count = visibility.shape[2]
    block_count, sub_u, block_width = kernel_rows.shape
    sub_v = kernel_cols.shape[1]
    station_rows = visibility.reshape(2, fine_local, block_count, block_width, station_count)
    partial_value = jnp.einsum(
        "iab,xfibs->xfias", kernel_rows, station_rows, preferred_element_type=jnp.float32
    )
    partial_value = partial_value.reshape(
        2, fine_local, block_count, sub_u, block_count, block_width
    )
    result = jnp.einsum(
        "xfiajc,jdc->xfijad",
        partial_value,
        kernel_cols.astype(jnp.float32),
        precision=lax.Precision.HIGHEST,
    )
    return result.reshape(2, fine_local, block_count * block_count, sub_u * sub_v).astype(
        jnp.bfloat16
    )


def fine_subgrids(spectra, kernel_rows, kernel_cols):

    def one_fine(spec_one):
        return subgrids(correlate(spec_one[None]), kernel_rows, kernel_cols)[:, 0]

    stacked = lax.map(one_fine, spectra)
    return jnp.transpose(stacked, (1, 0, 2, 3))


def phase_table(positions, offset_count, pixels, grid_size):
    offsets = jnp.arange(offset_count, dtype=jnp.int32)
    position = positions[:, None, None] + offsets[None, :, None]
    phase_turns = jnp.mod(position * pixels[None, None, :], grid_size)
    angles = phase_turns.astype(jnp.float32) * (2.0 * math.pi / grid_size)
    return (jnp.cos(angles).astype(jnp.bfloat16), jnp.sin(angles).astype(jnp.bfloat16))


def image_rows(subgrid, positions, row_count, row_total, sub_u, sub_v, col_total, grid_size):
    count_sub = subgrid.shape[1]
    row_pix = jnp.arange(row_count, dtype=jnp.int32) - row_total // 2
    col_pix = jnp.arange(col_total, dtype=jnp.int32) - col_total // 2
    row_cos, row_sin = phase_table(positions[0], sub_u, row_pix, grid_size)
    col_cos, col_sin = phase_table(positions[1], sub_v, col_pix, grid_size)
    sub_cells = subgrid.reshape(2, count_sub, sub_u, sub_v)
    proj_real = (
        jnp.einsum("nal,nab->nbl", row_cos, sub_cells[0], preferred_element_type=jnp.float32)
        - jnp.einsum("nal,nab->nbl", row_sin, sub_cells[1], preferred_element_type=jnp.float32)
    ).astype(jnp.bfloat16)
    proj_imag = (
        jnp.einsum("nal,nab->nbl", row_cos, sub_cells[1], preferred_element_type=jnp.float32)
        + jnp.einsum("nal,nab->nbl", row_sin, sub_cells[0], preferred_element_type=jnp.float32)
    ).astype(jnp.bfloat16)
    return jnp.einsum(
        "nbl,nbm->lm", proj_real, col_cos, preferred_element_type=jnp.float32
    ) - jnp.einsum("nbl,nbm->lm", proj_imag, col_sin, preferred_element_type=jnp.float32)


def local(voltages, station_flags, filter_taps, kernel_rows, kernel_cols, cell_index):
    spectra = channelize(voltages[0], station_flags, filter_taps)
    turned = lax.all_to_all(spectra, "turn", split_axis=0, concat_axis=2, tiled=True)
    subgrid = fine_subgrids(turned, kernel_rows[0], kernel_cols[0])
    sub_u = kernel_rows.shape[2]
    sub_v = kernel_cols.shape[2]
    block_count = kernel_rows.shape[1]
    device_total = lax.axis_size("role") * lax.axis_size("band") * lax.axis_size("turn")
    row_total = ROWS_DEV * device_total
    channel_total = FINE * lax.axis_size("role") * lax.axis_size("band")
    scale_factor = 4.0 / math.sqrt(channel_total * block_count * block_count * sub_u * sub_v)
    flat_grid = subgrid.reshape(2, -1, sub_u * sub_v)
    flat_places = cell_index.reshape(2, -1)
    summed = lax.psum_scatter(
        image_rows(
            flat_grid,
            flat_places,
            row_total // device_total * lax.axis_size(("role", "band", "turn")),
            row_total,
            sub_u,
            sub_v,
            MW,
            NGRID,
        ),
        ("role", "band", "turn"),
        scatter_dimension=0,
        tiled=True,
    )
    return summed * scale_factor


def solution(mesh):
    in_specs = (
        P(("role", "band"), None, "turn", None),
        P("turn"),
        P(),
        P(("role", "band"), None, None, None),
        P(("role", "band"), None, None, None),
        P(None, ("role", "band", "turn"), None),
    )
    out_specs = P(("role", "band", "turn"), None)
    return jax.shard_map(local, mesh=mesh, in_specs=in_specs, out_specs=out_specs, check_vma=False)
```

profile of v0, /device:TPU:0, one launch (start us, length us, event | category | flops | bytes accessed | tf_op | source)
XLA Modules:
  0.0 110.8 jit_solution(2292162804014548833)
XLA Ops:
  0.0 1.9 %squeeze.46 = bf16[128,15,256]{2,1,0:T(8,128)(2,1)S(1)} reshape(bf16[1,2,64,3840]{3,2,1,0:T(8,128)(2,1)} %param.8) | data formatting | bytes 1966080 | tf_op jit(solution)/shard_map/squeeze | solution.py:109
  2.2 1.0 copy-done
  5.9 1.6 %copy.16 = bf16[128,2,64,2,8]{2,4,3,1,0:T(8,128)(2,1)S(1)} copy(bf16[128,2,64,2,8]{0,4,3,2,1:T(8,128)(2,1)S(1)} %bitcast.134) | data formatting | bytes 1048576 | tf_op jit(solution)/shard_map/transpose | solution.py:31
  7.6 1.5 %reshape.208 = bf16[4,2,32768]{2,1,0:T(2,128)(2,1)} reshape(bf16[128,2,16,64]{3,2,1,0:T(8,128)(2,1)S(1)} %bitcast_bitcast_fusion) | data formatting | bytes 1048576
  9.2 4.2 %all-to-all-start = ((bf16[4,2,32768]{2,1,0:T(2,128)(2,1)}), bf16[4,2,32768]{2,1,0:T(2,128)(2,1)S(1)}, u32[]{:S(2)}, u32[]{:S(2)}) async-start(bf16[4,2,32768]{2,1,0:T(2,128)(2,1)} %reshape.208), calls=%async_computation | async-start | bytes 1048576 | tf_op jit(solution)/shard_map/all_to_all | solution.py:110
  13.4 0.7 copy-done.2
  14.2 8.1 %all-to-all-done = bf16[4,2,32768]{2,1,0:T(2,128)(2,1)S(1)} async-done(((bf16[4,2,32768]{2,1,0:T(2,128)(2,1)}), bf16[4,2,32768]{2,1,0:T(2,128)(2,1)S(1)}, u32[]{:S(2)}, u32[]{:S(2)}) %all-to-all-start) | async-done | bytes 524320 | tf_op jit(solution)/shard_map/all_to_all | solution.py:110
  22.2 0.7 reshape.209
  23.0 1.4 %copy.17 = bf16[32,2,4,64,16]{3,2,4,1,0:T(4,128)(2,1)S(1)} copy(bf16[32,2,4,64,16]{3,4,1,0,2:T(8,128)(2,1)S(1)} %bitcast.133) | data formatting | bytes 1048576 | tf_op jit(solution)/shard_map/all_to_all | solution.py:110
  24.3 0.7 all_to_all.16
  25.1 31.0 %while.10 = (s32[]{:T(128)}, bf16[32,2,1,1024]{3,1,2,0:T(2,128)(2,1)S(1)}, bf16[32,2,256,16]{2,3,1,0:T(8,128)(2,1)S(1)}, bf16[1,32,256]{2,1,0:T(8,128)(2,1)S(1)}...) while((s32[]{:T(128)}, bf16[32,2,1,1024]{3,1,2,0:T(2,128)(2,1)S(1)}, ...), condition=%wide.region_1.2_spmd, body=%wide.region_0.1_spmd.sunk | while | flops 24098820 | bytes 3428465 | solution.py:76
  26.0 0.3 convolution_bitcast_fusion.4
  27.0 0.3 convolution_bitcast_fusion.4
  28.0 0.3 convolution_bitcast_fusion.4
  29.0 0.3 convolution_bitcast_fusion.4
  29.9 0.3 convolution_bitcast_fusion.4
  30.9 0.3 convolution_bitcast_fusion.4
  31.9 0.3 convolution_bitcast_fusion.4
  32.8 0.3 convolution_bitcast_fusion.4
  33.8 0.3 convolution_bitcast_fusion.4
  34.8 0.3 convolution_bitcast_fusion.4
  35.7 0.3 convolution_bitcast_fusion.4
  36.7 0.3 convolution_bitcast_fusion.4
  37.7 0.3 convolution_bitcast_fusion.4
  39.6 0.3 convolution_bitcast_fusion.4
  40.6 0.3 convolution_bitcast_fusion.4
  41.5 0.3 convolution_bitcast_fusion.4
  42.5 0.3 convolution_bitcast_fusion.4
  43.5 0.3 convolution_bitcast_fusion.4
  44.4 0.3 convolution_bitcast_fusion.4
  45.4 0.3 convolution_bitcast_fusion.4
  46.4 0.3 convolution_bitcast_fusion.4
  47.4 0.3 convolution_bitcast_fusion.4
  48.3 0.3 convolution_bitcast_fusion.4
  49.3 0.3 convolution_bitcast_fusion.4
  50.3 0.3 convolution_bitcast_fusion.4
  51.2 0.3 convolution_bitcast_fusion.4
  52.2 0.3 convolution_bitcast_fusion.4
  53.2 0.3 convolution_bitcast_fusion.4
  54.1 0.3 convolution_bitcast_fusion.4
  55.1 0.3 convolution_bitcast_fusion.4
  56.0 0.5 slice_reduce_fusion
  56.9 2.4 %fusion.34 = f32[32,32,32]{2,1,0:T(8,128)S(1)} fusion(bf16[32,32,32]{2,1,0:T(8,128)(2,1)S(1)} %squeeze.57, s32[32]{0:T(128)S(1)} %iota_add_fusion.3, s32[32,32]{1,0:T(8,128)S(1)} %get-tuple-element.52), kind=kOutput, calls=%fused_computation.73 | convolution fusion | flops 2588672 | bytes 200832 | tf_op jit(solution)/shard_map/nal,nab->nbl/dot_general | solution.py:96
  59.3 2.4 %fusion.33 = f32[32,32,32]{2,1,0:T(8,128)S(1)} fusion(bf16[32,32,32]{2,1,0:T(8,128)(2,1)S(1)} %squeeze.58, s32[32]{0:T(128)S(1)} %iota_add_fusion.3, s32[32,32]{1,0:T(8,128)S(1)} %get-tuple-element.52), kind=kOutput, calls=%fused_computation.72 | convolution fusion | flops 2588672 | bytes 200832 | tf_op jit(solution)/shard_map/nal,nab->nbl/dot_general | solution.py:100
  61.8 4.1 %fusion.21 = f32[32,128]{1,0:T(8,128)S(1)} fusion(f32[32,32,32]{2,1,0:T(8,128)S(1)} %fusion.34, bf16[32,32,32]{2,1,0:T(8,128)(2,1)S(1)} %squeeze.58, s32[128]{0:T(128)S(1)} %iota_add_fusion.2, s32[32,32]{1,0:T(8,128)S(1)} %get-tuple-element.51, s32[32]{0:T(128)S(1)} %iota_add_fusion.3, s32[32,32]{1,0:T(8,128)S(1)} %get-tuple-element.52), kind=kOutput, calls=%fused_computation.39 | convolution fusion | flops 13008896 | bytes 221824 | tf_op jit(solution)/shard_map/nbl,nbm->lm/dot_general | solution.py:103
  65.9 4.1 %fusion.23 = f32[32,128]{1,0:T(8,128)S(1)} fusion(f32[32,128]{1,0:T(8,128)S(1)} %fusion.21, f32[32,32,32]{2,1,0:T(8,128)S(1)} %fusion.33, bf16[32,32,32]{2,1,0:T(8,128)(2,1)S(1)} %squeeze.57, s32[128]{0:T(128)S(1)} %iota_add_fusion.2, s32[32,32]{1,0:T(8,128)S(1)} %get-tuple-element.51, s32[32]{0:T(128)S(1)} %iota_add_fusion.3, ...), kind=kOutput, calls=%fused_computation.41 | convolution fusion | flops 13012992 | bytes 238208 | tf_op jit(solution)/shard_map/nbl,nbm->lm/dot_general | solution.py:105
  70.0 40.3 %all-reduce = f32[32,128]{1,0:T(8,128)S(1)} all-reduce(f32[32,128]{1,0:T(8,128)S(1)} %fusion.23), channel_id=2, replica_groups=mesh['role'=2,'band'=4,'turn'=4] {'role','band','turn'}, use_global_device_ids=true, to_apply=%region_2.3.clone | all-reduce | flops 4096 | bytes 32768
  110.3 0.5 dynamic-slice_multiply_fusion
  (286 shorter events, 22.7 us)
Async XLA Ops:
  0.0 1.9 %copy-start.4 = (s32[64]{0:T(128)S(1)}, s32[64]{0:T(128)}, u32[]{:S(2)}) copy-start(s32[64]{0:T(128)} %param.9) | copy-start | bytes 772
  2.0 1.2 %copy-start = (bf16[8,256,256]{2,1,0:T(8,128)(2,1)S(1)}, bf16[8,256,256]{2,1,0:T(8,128)(2,1)}, u32[]{:S(2)}) copy-start(bf16[8,256,256]{2,1,0:T(8,128)(2,1)} %param.10) | copy-start | bytes 3145732
  9.2 13.1 %all-to-all-start = ((bf16[4,2,32768]{2,1,0:T(2,128)(2,1)}), bf16[4,2,32768]{2,1,0:T(2,128)(2,1)S(1)}, u32[]{:S(2)}, u32[]{:S(2)}) async-start(bf16[4,2,32768]{2,1,0:T(2,128)(2,1)} %reshape.208), calls=%async_computation | async-start | bytes 1048576 | tf_op jit(solution)/shard_map/all_to_all | solution.py:110
  13.4 0.7 copy-start.2
  24.3 0.7 copy-start.1
  24.3 0.7 copy-start.3
where the time goes:
time: 111 us
  blocking collectives  40.3 us (36%)
  matrix products  36.6 us (33%)
  local copies, waits for them, and re-layouts  15 us (14%)
  waiting for transfers between devices  8.07 us (7%)
  other arithmetic  4.98 us (4%)
  starting transfers between devices  4.21 us (4%)
  loops' own time  1.52 us (1%)
    unnamed x1, blocking collectives  40.3 us
    dot_general x32, matrix products, correlate(): jnp.einsum('fpsa,fpka->fpsk', spectra, stacked, preferred_element_type=jn...  10.9 us
    all_to_all x1, waiting for transfers between devices, local(): lax.all_to_all(spectra, 'turn', split_axis=0, concat_axis=2, tiled=True)  8.07 us
    dot_general x32, matrix products, subgrids(): jnp.einsum('xfiajc,jdc->xfijad', partial_value, kernel_cols.astype(jnp.fl...  5.31 us
    dot_general x32, matrix products, subgrids(): jnp.einsum('iab,xfibs->xfias', kernel_rows, station_rows, preferred_eleme...  4.73 us
    all_to_all x1, starting transfers between devices, local(): lax.all_to_all(spectra, 'turn', split_axis=0, concat_axis=2, tiled=True)  4.21 us
    dot_general x1, matrix products, image_rows(): jnp.einsum('nbl,nbm->lm', proj_imag, col_sin, preferred_element_type=jnp....  4.15 us
    unnamed x13, local copies, waits for them, and re-layouts  4.13 us
  transfers between devices with their start and end apart: 1, of which 1 were waited for; matrix products, arithmetic and copies ran while one was open for 0% of the time, Pallas kernels for 0%

commit v1 on v0

v1 whole, which is shorter than its diff:
```python
import functools
import math

import jax
import jax.numpy as jnp
import numpy as np
from jax import lax
from jax.experimental import pallas as pl
from jax.experimental.pallas import tpu as pltpu
from jax.sharding import PartitionSpec as P

NGRID = 4096
MW = 128
ROWS_DEV = 1
DIGIT = 64
PAD_ROWS = 16
VMEM_BYTES = 40 * 1024 * 1024


def spectra_kernel(pairs_each, volt_ref, flag_ref, taps_ref, rows_ref, cols_ref, cell_ref, out_ref):
    turn = lax.axis_index("turn")
    _, station_rows, width = volt_ref.shape
    taps, two_fine, _ = taps_ref.shape
    frames = width // two_fine - taps + 1
    dests = out_ref.shape[0]
    both = jnp.concatenate([rows_ref[...], cols_ref[...]], axis=0).astype(jnp.float32)
    weights = jnp.zeros((both.shape[0], station_rows), jnp.float32)
    for group in range(dests):
        piece = both[:, group * station_rows : (group + 1) * station_rows]
        weights = jnp.where(turn == group, piece, weights)
    weights = (weights * flag_ref[...].astype(jnp.float32)).astype(jnp.bfloat16)

    filt = taps_ref[...].reshape(taps * two_fine, two_fine)
    cells_rows = both.shape[0]
    for dest in range(dests):
        pairs = range(dest * pairs_each, (dest + 1) * pairs_each)
        lhs = jnp.concatenate(
            [
                volt_ref[pair // frames, :, (pair % frames) * two_fine : (pair % frames + taps) * two_fine]
                for pair in pairs
            ],
            axis=0,
        )
        spectra = jnp.dot(lhs, filt, preferred_element_type=jnp.float32).astype(jnp.bfloat16)
        for index in range(pairs_each):
            gridded = jnp.dot(
                weights,
                spectra[index * station_rows : (index + 1) * station_rows],
                preferred_element_type=jnp.float32,
            )
            out_ref[dest, index * cells_rows : (index + 1) * cells_rows] = gridded.astype(jnp.bfloat16)

    cell = cell_ref[...]
    count = cell.shape[1]
    wide = jnp.concatenate([cell] * (two_fine // count), axis=1)
    lane = lax.broadcasted_iota(jnp.int32, wide.shape, 1)
    wide = jnp.where((lane >= turn * count) & (lane < (turn + 1) * count), wide, 0)
    digits = jnp.concatenate([wide // DIGIT, wide % DIGIT], axis=0).astype(jnp.float32)
    digits = jnp.concatenate([digits, jnp.zeros((PAD_ROWS - 4, two_fine), jnp.float32)], axis=0)
    for dest in range(dests):
        out_ref[dest, pairs_each * cells_rows :] = digits.astype(jnp.bfloat16)


def image_kernel(pairs_each, row_total, got_ref, row_dft_ref, col_dft_ref, out_ref):
    fine = got_ref.shape[2] // 2
    sub = row_dft_ref.shape[1] // 4
    total = got_ref[0].astype(jnp.float32)
    for source in range(1, got_ref.shape[0]):
        total = total + got_ref[source].astype(jnp.float32)
    digits = total[pairs_each * 2 * sub :]
    cell_u = (digits[0:1, :fine] * DIGIT + digits[2:3, :fine]).astype(jnp.int32)
    cell_v = (digits[1:2, :fine] * DIGIT + digits[3:4, :fine]).astype(jnp.int32)

    def phase(cell, count):
        pixel = lax.broadcasted_iota(jnp.int32, (count, fine), 0) - count // 2
        angle = ((cell * pixel) & (NGRID - 1)).astype(jnp.float32) * (2.0 * math.pi / NGRID)
        return jnp.cos(angle), jnp.sin(angle)

    def transform(dft_ref, first, cos, sin):
        held = jnp.concatenate(
            [
                jnp.concatenate(
                    [
                        total[index * 2 * sub + first : index * 2 * sub + first + sub, :fine],
                        total[index * 2 * sub + first : index * 2 * sub + first + sub, fine:],
                    ],
                    axis=0,
                )
                for index in range(pairs_each)
            ],
            axis=1,
        ).astype(jnp.bfloat16)
        plain = jnp.dot(dft_ref[...], jnp.concatenate([held, held], axis=0), preferred_element_type=jnp.float32)
        half = plain.shape[0] // 2
        real, imag = plain[:half], plain[half:]
        cos = jnp.concatenate([cos] * pairs_each, axis=1)
        sin = jnp.concatenate([sin] * pairs_each, axis=1)
        return real * cos - imag * sin, real * sin + imag * cos

    row_real, row_imag = transform(row_dft_ref, 0, *phase(cell_u, row_total))
    col_real, col_imag = transform(col_dft_ref, sub, *phase(cell_v, MW))
    left = jnp.concatenate([row_real, -row_imag], axis=1).astype(jnp.bfloat16)
    right = jnp.concatenate([col_real, col_imag], axis=1).astype(jnp.bfloat16)
    out_ref[...] = lax.dot_general(
        left, right, (((1,), (1,)), ((), ())), preferred_element_type=jnp.float32
    )


def dft_matrix(pixels, cells, conjugate):
    angle = 2.0 * np.pi / NGRID * np.outer(np.arange(pixels) - pixels // 2, np.arange(cells))
    cos, sin = np.cos(angle), np.sin(angle)
    sign = -1.0 if conjugate else 1.0
    whole = np.block([[cos, -sign * sin], [sin, sign * cos]]).astype(np.float32)
    high = whole.astype(jnp.bfloat16)
    low = (whole - high.astype(np.float32)).astype(jnp.bfloat16)
    return np.concatenate([high, low], axis=1)


def call(kernel, out_shape, args):
    return pl.pallas_call(
        kernel,
        out_shape=out_shape,
        in_specs=[pl.BlockSpec(memory_space=pltpu.VMEM)] * len(args),
        out_specs=pl.BlockSpec(memory_space=pltpu.VMEM),
        compiler_params=pltpu.CompilerParams(vmem_limit_bytes=VMEM_BYTES),
    )(*args)


def local(voltages, station_flags, filter_taps, kernel_rows, kernel_cols, cell_index):
    polars, _, width = voltages.shape[1:]
    taps, two_fine, _ = filter_taps.shape
    sub_u, sub_v = kernel_rows.shape[2], kernel_cols.shape[2]
    turns = lax.axis_size("turn")
    everyone = ("role", "band", "turn")
    row_total = ROWS_DEV * lax.axis_size(everyone)
    channels = two_fine // 2 * lax.axis_size("role") * lax.axis_size("band")
    frames = width // two_fine - taps + 1
    scale_factor = 4.0 / math.sqrt(channels * sub_u * sub_v) / frames
    pairs_each = polars * frames // turns
    sent_rows = pairs_each * (sub_u + sub_v) + PAD_ROWS

    sent = call(
        functools.partial(spectra_kernel, pairs_each),
        jax.ShapeDtypeStruct((turns, sent_rows, two_fine), jnp.bfloat16),
        (
            voltages[0],
            station_flags.reshape(1, -1),
            filter_taps,
            kernel_rows[0, 0],
            kernel_cols[0, 0],
            cell_index.reshape(2, -1),
        ),
    )
    got = lax.all_to_all(sent, "turn", split_axis=0, concat_axis=0, tiled=True)
    part = call(
        functools.partial(image_kernel, pairs_each, row_total),
        jax.ShapeDtypeStruct((row_total, MW), jnp.float32),
        (
            got,
            jnp.asarray(dft_matrix(row_total, sub_u, False)),
            jnp.asarray(dft_matrix(MW, sub_v, True)),
        ),
    )
    rows = lax.all_to_all(part, everyone, split_axis=0, concat_axis=0, tiled=True)
    return jnp.sum(rows.reshape(-1, ROWS_DEV, MW), axis=0) * scale_factor


def solution(mesh):
    in_specs = (
        P(("role", "band"), None, "turn", None),
        P("turn"),
        P(),
        P(("role", "band"), None, None, None),
        P(("role", "band"), None, None, None),
        P(None, ("role", "band", "turn"), None),
    )
    out_specs = P(("role", "band", "turn"), None)
    return jax.shard_map(local, mesh=mesh, in_specs=in_specs, out_specs=out_specs, check_vma=False)
```

time: 111 us -> 34.2 us (0.31)
  matrix products: 36.6 us -> 0 us
  blocking collectives: 40.3 us -> 25.2 us
  local copies, waits for them, and re-layouts: 15 us -> 4.55 us
  waiting for transfers between devices: 8.07 us -> 0 us
  other arithmetic: 4.98 us -> 0.57 us
  starting transfers between devices: 4.21 us -> 0 us
  Pallas kernels: 0 us -> 3.39 us
  loops' own time: 1.52 us -> 0 us
    unnamed x1 -> x0, blocking collectives: 40.3 us -> none
    dot_general x108 -> x0, matrix products: 36.6 us -> none  [the longest x32 10.9 us: correlate(): jnp.einsum('fpsa,fpka->fpsk', spectra, stacked, preferred_element_type=jn...]
    all_to_all x0 -> x2, blocking collectives: none -> 25.2 us  [the longest x1 13.3 us: local(): got = lax.all_to_all(sent, 'turn', split_axis=0, concat_axis=0, tiled=True)]
    all_to_all x1 -> x0, waiting for transfers between devices: 8.07 us -> none  [local(): lax.all_to_all(spectra, 'turn', split_axis=0, concat_axis=2, tiled=True)]
    all_to_all x1 -> x0, starting transfers between devices: 4.21 us -> none  [local(): lax.all_to_all(spectra, 'turn', split_axis=0, concat_axis=2, tiled=True)]
    another operation x32 -> x0, other arithmetic: 3.76 us -> none
    pallas_call x0 -> x2, Pallas kernels: none -> 3.39 us  [call(): pl.pallas_call(kernel, out_shape=out_shape, in_specs=[pl.BlockSpec(memory...]
    convert_element_type x32 -> x0, local copies, waits for them, and re-layouts: 2.88 us -> none  [subgrids(): result.reshape(2, fine_local, block_count * block_count, sub_u * sub_v)]
  transfers between devices with their start and end apart: 1 -> 0, of which waited for: 1 -> 0; matrix products, arithmetic and copies ran while one was open for 0% -> 0% of each run, Pallas kernels for 0% -> 0%
where the time goes in v1:
time: 34.2 us; the launch traced here: 33.8 us
  blocking collectives  25.2 us (74%)
  local copies, waits for them, and re-layouts  4.55 us (13%)
  Pallas kernels  3.39 us (10%)
  other arithmetic  0.57 us (2%)
    all_to_all x1, blocking collectives, local(): got = lax.all_to_all(sent, 'turn', split_axis=0, concat_axis=0, tiled=True)  13.3 us
    all_to_all x1, blocking collectives, local(): lax.all_to_all(part, everyone, split_axis=0, concat_axis=0, tiled=True)  11.9 us
    unnamed x16, local copies, waits for them, and re-layouts  4.55 us
    pallas_call x2, Pallas kernels, call(): pl.pallas_call(kernel, out_shape=out_shape, in_specs=[pl.BlockSpec(memory...  3.39 us

profile of v1, /device:TPU:0, one launch (start us, length us, event | category | flops | bytes accessed | tf_op | source)
XLA Modules:
  0.0 33.8 jit_solution(14234960099633497528)
XLA Ops:
  0.0 0.0 copy-start.6
  0.0 0.0 copy-start.7
  0.0 0.7 %copy-done.6 = s32[2,32,1]{1,2,0:T(1,128)S(1)} copy-done((s32[2,32,1]{1,2,0:T(1,128)S(1)}, s32[2,32,1]{1,2,0:T(1,128)}, u32[]{:S(2)}) %copy-start.6) | copy-done | bytes 280
  0.7 0.0 copy-done.7
  0.7 0.0 copy-start
  0.7 1.2 %copy-done = bf16[8,256,256]{2,1,0:T(8,128)(2,1)S(1)} copy-done((bf16[8,256,256]{2,1,0:T(8,128)(2,1)S(1)}, bf16[8,256,256]{2,1,0:T(8,128)(2,1)}, u32[]{:S(2)}) %copy-start) | copy-done | bytes 1048600
  1.9 0.0 copy-start.1
  1.9 1.2 %copy-done.1 = bf16[1,2,64,3840]{3,2,1,0:T(8,128)(2,1)S(1)} copy-done((bf16[1,2,64,3840]{3,2,1,0:T(8,128)(2,1)S(1)}, bf16[1,2,64,3840]{3,2,1,0:T(8,128)(2,1)}, u32[]{:S(2)}) %copy-start.1) | copy-done | bytes 983064
  3.1 0.0 copy-start.3
  3.1 0.7 %copy-done.3 = bf16[1,1,32,256]{3,2,1,0:T(8,128)(2,1)S(1)} copy-done((bf16[1,1,32,256]{3,2,1,0:T(8,128)(2,1)S(1)}, bf16[1,1,32,256]{3,2,1,0:T(8,128)(2,1)}, u32[]{:S(2)}) %copy-start.3) | copy-done | bytes 16408
  3.8 0.0 copy-start.4
  3.8 0.7 %copy-done.4 = bf16[1,1,32,256]{3,2,1,0:T(8,128)(2,1)S(1)} copy-done((bf16[1,1,32,256]{3,2,1,0:T(8,128)(2,1)S(1)}, bf16[1,1,32,256]{3,2,1,0:T(8,128)(2,1)}, u32[]{:S(2)}) %copy-start.4) | copy-done | bytes 16408
  4.5 2.7 %shard_map.82 = bf16[4,272,256]{2,1,0:T(8,128)(2,1)S(1)} custom-call(bf16[2,64,3840]{2,1,0:T(8,128)(2,1)S(1)} %bitcast.10, s32[1,64]{1,0:T(1,128)S(1)} %bitcast.15, bf16[8,256,256]{2,1,0:T(8,128)(2,1)S(1)} %copy-done, bf16[32,256]{1,0:T(8,128)(2,1)S(1)} %bitcast.12, bf16[32,256]{1,0:T(8,128)(2,1)S(1)} %bitcast.13, s32[2,32]{1,0:T(2,128)S(1)} %bitcast.14), custom_call_target="tpu_custom_call" | custom-call | tf_op jit(solution)/shard_map/pallas_call | solution.py:120
  7.3 0.0 copy-start.2
  7.3 0.0 copy-start.5
  7.3 13.3 %all_to_all.14.got_ref = bf16[4,272,256]{2,1,0:T(8,128)(2,1)S(1)} all-to-all(bf16[4,272,256]{2,1,0:T(8,128)(2,1)S(1)} %shard_map.82), channel_id=1, replica_groups=mesh['role'=2,'band'=4,'turn'=4] {'turn'}, dimensions={0} | all-to-all | bytes 1114112 | tf_op jit(solution)/shard_map/all_to_all | solution.py:154
  20.7 0.0 copy-done.2
  20.7 0.0 copy-done.5
  20.7 0.6 %shard_map.83 = f32[32,128]{1,0:T(8,128)S(1)} custom-call(bf16[4,272,256]{2,1,0:T(8,128)(2,1)S(1)} %all_to_all.14.got_ref, bf16[64,128]{1,0:T(8,128)(2,1)S(1)} %copy-done.5, bf16[256,128]{1,0:T(8,128)(2,1)S(1)} %copy-done.2), custom_call_target="tpu_custom_call" | custom-call | tf_op jit(solution)/shard_map/pallas_call | solution.py:120
  21.3 11.9 %all_to_all.15 = f32[32,1,128]{2,1,0:T(1,128)S(1)} all-to-all(f32[32,1,128]{2,1,0:T(1,128)S(1)} %bitcast.11), channel_id=1, replica_groups=mesh['role'=2,'band'=4,'turn'=4] {'role','band','turn'}, dimensions={0} | all-to-all | bytes 32768 | tf_op jit(solution)/shard_map/all_to_all | solution.py:164
  33.2 0.1 reduce_sum.9
  33.3 0.5 %multiply_bitcast_fusion = f32[1,128]{1,0:T(1,128)} fusion(f32[128]{0:T(128)S(1)} %reduce_sum.9), kind=kLoop, calls=%fused_computation | loop fusion | flops 128 | bytes 1024 | tf_op jit(solution)/shard_map/mul | solution.py:165
Async XLA Ops:
  0.0 0.7 %copy-start.6 = (s32[2,32,1]{1,2,0:T(1,128)S(1)}, s32[2,32,1]{1,2,0:T(1,128)}, u32[]{:S(2)}) copy-start(s32[2,32,1]{1,2,0:T(1,128)} %param.13) | copy-start | bytes 772
  0.0 0.7 %copy-start.7 = (s32[64]{0:T(128)S(1)}, s32[64]{0:T(128)}, u32[]{:S(2)}) copy-start(s32[64]{0:T(128)} %param.9) | copy-start | bytes 772
  0.7 1.2 %copy-start = (bf16[8,256,256]{2,1,0:T(8,128)(2,1)S(1)}, bf16[8,256,256]{2,1,0:T(8,128)(2,1)}, u32[]{:S(2)}) copy-start(bf16[8,256,256]{2,1,0:T(8,128)(2,1)} %taps_ref.1) | copy-start | bytes 3145732
  1.9 1.2 %copy-start.1 = (bf16[1,2,64,3840]{3,2,1,0:T(8,128)(2,1)S(1)}, bf16[1,2,64,3840]{3,2,1,0:T(8,128)(2,1)}, u32[]{:S(2)}) copy-start(bf16[1,2,64,3840]{3,2,1,0:T(8,128)(2,1)} %param.8) | copy-start | bytes 2949124
  3.1 0.7 %copy-start.3 = (bf16[1,1,32,256]{3,2,1,0:T(8,128)(2,1)S(1)}, bf16[1,1,32,256]{3,2,1,0:T(8,128)(2,1)}, u32[]{:S(2)}) copy-start(bf16[1,1,32,256]{3,2,1,0:T(8,128)(2,1)} %param.11) | copy-start | bytes 49156
  3.8 0.7 %copy-start.4 = (bf16[1,1,32,256]{3,2,1,0:T(8,128)(2,1)S(1)}, bf16[1,1,32,256]{3,2,1,0:T(8,128)(2,1)}, u32[]{:S(2)}) copy-start(bf16[1,1,32,256]{3,2,1,0:T(8,128)(2,1)} %param.12) | copy-start | bytes 49156
  7.3 13.4 %copy-start.2 = (bf16[256,128]{1,0:T(8,128)(2,1)S(1)}, bf16[256,128]{1,0:T(8,128)(2,1)}, u32[]{:S(2)}) copy-start(bf16[256,128]{1,0:T(8,128)(2,1)} %constant.9.clone.col_dft_ref) | copy-start | bytes 196612
  7.3 13.4 %copy-start.5 = (bf16[64,128]{1,0:T(8,128)(2,1)S(1)}, bf16[64,128]{1,0:T(8,128)(2,1)}, u32[]{:S(2)}) copy-start(bf16[64,128]{1,0:T(8,128)(2,1)} %constant.8.clone.row_dft_ref) | copy-start | bytes 49156
